TPU v7x, 32 devices: a whole 2x2x4 slice. The times are simulated.
32 devices in a mesh: patch: 8 (over z, y), sub: 4 (over x, core).
Axes of the slice: x: 2, y: 2, z: 4, core: 2. Of those that a mesh axis runs over, the one named last changes fastest.
Arguments:
- fine_nodes: bfloat16 [16384, 512], P(('patch', 'sub')), may hold values from -6 to 6
- coarse_nodes: bfloat16 [128, 512], replicated, may hold values from -6 to 6
- neighbours: int32 [6, 16384], P(None, ('patch', 'sub')), may hold values from 0 to 768, as said below
- send_rows: int32 [32, 2, 128], P(('patch', 'sub')), may hold values from 0 to 511, as said below
- real_rows: int32 [32], P(('patch', 'sub')), may hold values from 256 to 512
- parent: int32 [16384], P(('patch', 'sub')), may hold values from 0 to 127
- coarse_edges: int32 [2, 4096], P(None, ('patch', 'sub')), may hold values from 0 to 127
- coarse_live: int32 [32], P(('patch', 'sub')), may hold values from 32 to 128
- msg_weight: bfloat16 [1024, 512], replicated, may hold values from -0.1875 to 0.1875
- msg_bias: float32 [512], replicated, may hold values from -3 to 3
- node_weight: bfloat16 [1536, 512], replicated, may hold values from -0.15625 to 0.15625
- node_bias: float32 [512], replicated, may hold values from -3 to 3
- coarse_msg_weight: bfloat16 [1024, 512], replicated, may hold values from -0.1875 to 0.1875
- coarse_msg_bias: float32 [512], replicated, may hold values from -3 to 3
- coarse_node_weight: bfloat16 [1024, 512], replicated, may hold values from -0.1875 to 0.1875
- coarse_node_bias: float32 [512], replicated, may hold values from -3 to 3
- out_grad: bfloat16 [16384, 512], P(('patch', 'sub')), may hold values from -6 to 6
Outputs:
- new_fine: bfloat16 [16384, 512], P(('patch', 'sub'))
- new_coarse: bfloat16 [128, 512], replicated
- node_grad: bfloat16 [16384, 512], P(('patch', 'sub'))
- msg_weight_grad: float32 [1024, 512], replicated
Inputs may be any that keep to these rules, and one draw needn't show every extreme that they name: `neighbours`: entry [k, i] of device d is a real local row below real_rows[d], 512 + j for row j of the 128 received from the previous device, 640 + j for row j of those from the next one, or 768 for an empty slot. Padding rows have only empty slots, and every real row has 4 or more filled slots. `send_rows`: each entry is a real row of the sending device; rows may repeat.
All inputs are finite; a program needn't handle non-finite values.
Results may differ from a plain program's by a relative error of at most 0.0071.
Values may be sent and summed in bfloat16 or wider, within the bound.
A program may use at most 64 MiB of HBM per device.

v0:
```python
import jax
import jax.numpy as jnp
from jax import lax
from jax.sharding import PartitionSpec as P

WIDTH = 512


epsilon = 1e-06


def extended(x, sides, width):
    for axis, dim in sides:
        peers, length = (lax.axis_size(axis), x.shape[dim])
        up = [(i, (i + 1) % peers) for i in range(peers)]
        down = [(j, i) for i, j in up]
        last = lax.slice_in_dim(x, length - width, length, axis=dim)
        first = lax.slice_in_dim(x, 0, width, axis=dim)
        before = lax.ppermute(last, axis, up)
        after = lax.ppermute(first, axis, down)
        x = jnp.concatenate([before, x, after], axis=dim)
    return x


def slope(values):
    sigmoid_part = jax.nn.sigmoid(values)
    return sigmoid_part * (1.0 + values * (1.0 - sigmoid_part))


def coarse_finish(own_coarse, summed, coarse_node_weight, coarse_node_bias):
    hidden = (
        jnp.dot(
            jnp.concatenate([own_coarse, summed], 1),
            coarse_node_weight,
            preferred_element_type=jnp.float32,
        )
        + coarse_node_bias
    )
    return (own_coarse.astype(jnp.float32) + jax.nn.silu(hidden)).astype(jnp.bfloat16)


def transposed_product(left, right):
    return lax.dot_general(
        left, right, (((1,), (1,)), ((), ())), preferred_element_type=jnp.float32
    )


def shards(
    fine_nodes,
    coarse_nodes,
    neighbours,
    send_rows,
    real_rows,
    parent,
    coarse_edges,
    coarse_live,
    msg_weight,
    msg_bias,
    node_weight,
    node_bias,
    coarse_msg_weight,
    coarse_msg_bias,
    coarse_node_weight,
    coarse_node_bias,
    out_grad,
):
    node_count = fine_nodes.shape[0]
    send_count = send_rows.shape[2]
    coarse_count = coarse_nodes.shape[0]
    slot_count = coarse_edges.shape[1]
    table_rows = node_count + 2 * send_count
    senders = jnp.take(coarse_nodes, coarse_edges[0], axis=0)
    receivers = jnp.take(coarse_nodes, coarse_edges[1], axis=0)
    coarse_pre = (
        jnp.dot(
            jnp.concatenate([senders, receivers], 1),
            coarse_msg_weight,
            preferred_element_type=jnp.float32,
        )
        + coarse_msg_bias
    )
    usable = (jnp.arange(slot_count, dtype=jnp.int32) < coarse_live[0]).astype(jnp.float32)
    message = (jax.nn.silu(coarse_pre) * usable[:, None]).astype(jnp.bfloat16)
    picker = (
        coarse_edges[1][None, :] == jnp.arange(coarse_count, dtype=jnp.int32)[:, None]
    ).astype(jnp.bfloat16)
    partial_sum = jnp.dot(picker, message, preferred_element_type=jnp.float32)
    summed = lax.psum(partial_sum, ("patch", "sub")).astype(jnp.bfloat16)
    new_coarse = coarse_finish(coarse_nodes, summed, coarse_node_weight, coarse_node_bias)
    outgoing = jnp.take(fine_nodes, send_rows[0].reshape(-1), axis=0)
    rim_rows = extended(outgoing, ((("patch", "sub"), 0),), send_count)
    lookup = jnp.concatenate([fine_nodes, rim_rows[:send_count], rim_rows[3 * send_count :]], 0)
    source_weight = msg_weight[:WIDTH]
    target_weight = msg_weight[WIDTH:]
    source_proj = jnp.dot(lookup, source_weight, preferred_element_type=jnp.float32)
    source_proj = jnp.concatenate([source_proj, jnp.zeros((1, WIDTH), jnp.float32)], 0)
    target_proj = jnp.dot(fine_nodes, target_weight, preferred_element_type=jnp.float32)
    edge_pre = jnp.take(source_proj, neighbours, axis=0) + target_proj[None] + msg_bias
    filled = (neighbours < table_rows).astype(jnp.float32)[..., None]
    aggregated = jnp.sum(jax.nn.silu(edge_pre) * filled, axis=0).astype(jnp.bfloat16)
    lifted = jnp.take(new_coarse, parent, axis=0)
    is_real = (jnp.arange(node_count, dtype=jnp.int32) < real_rows[0])[:, None]
    joined = jnp.concatenate([fine_nodes, aggregated, lifted], 1)
    node_pre = jnp.dot(joined, node_weight, preferred_element_type=jnp.float32) + node_bias
    new_fine = jnp.where(
        is_real, fine_nodes.astype(jnp.float32) + jax.nn.silu(node_pre), 0.0
    ).astype(jnp.bfloat16)
    node_delta = jnp.where(is_real, out_grad.astype(jnp.float32) * slope(node_pre), 0.0).astype(
        jnp.bfloat16
    )
    node_back = transposed_product(node_delta, node_weight)
    edge_delta = (node_back[None, :, WIDTH : 2 * WIDTH] * slope(edge_pre) * filled).astype(
        jnp.bfloat16
    )
    delta_sum = jnp.sum(edge_delta.astype(jnp.float32), axis=0).astype(jnp.bfloat16)
    flat_delta = edge_delta.reshape(-1, WIDTH)
    table_picker = (
        neighbours.reshape(-1)[None, :] == jnp.arange(table_rows, dtype=jnp.int32)[:, None]
    ).astype(jnp.bfloat16)
    table_delta = jnp.dot(table_picker, flat_delta, preferred_element_type=jnp.float32).astype(
        jnp.bfloat16
    )
    table_grad = transposed_product(table_delta, source_weight)
    own_table_grad = table_grad[:node_count]
    back_rim = extended(
        table_grad[node_count:].astype(jnp.bfloat16), ((("patch", "sub"), 0),), send_count
    ).astype(jnp.float32)
    from_prev_grad = back_rim[:send_count]
    from_next_grad = back_rim[3 * send_count :]
    returned = jnp.zeros((node_count, WIDTH), jnp.float32)
    returned = (
        returned.at[send_rows[0, 0]].add(from_prev_grad).at[send_rows[0, 1]].add(from_next_grad)
    )
    target_back = transposed_product(delta_sum, target_weight)
    local_grad = (
        out_grad.astype(jnp.float32)
        + node_back[:, :WIDTH]
        + target_back
        + own_table_grad
        + returned
    )
    node_grad = jnp.where(is_real, local_grad, 0.0).astype(jnp.bfloat16)
    grad_source = lax.dot_general(
        lookup, table_delta, (((0,), (0,)), ((), ())), preferred_element_type=jnp.float32
    )
    grad_target = lax.dot_general(
        fine_nodes, delta_sum, (((0,), (0,)), ((), ())), preferred_element_type=jnp.float32
    )
    partial_grad = jnp.concatenate([grad_source, grad_target], 0)
    raw_grad = lax.psum(partial_grad, ("patch", "sub"))
    factor = lax.rsqrt(jnp.mean(raw_grad * raw_grad) + epsilon)
    msg_weight_grad = raw_grad * factor
    return (new_fine, new_coarse, node_grad, msg_weight_grad)


def solution(mesh):
    placed = (
        P(("patch", "sub"), None),
        P(),
        P(None, ("patch", "sub")),
        P(("patch", "sub"), None, None),
        P(("patch", "sub")),
        P(("patch", "sub")),
        P(None, ("patch", "sub")),
        P(("patch", "sub")),
        P(),
        P(),
        P(),
        P(),
        P(),
        P(),
        P(),
        P(),
        P(("patch", "sub"), None),
    )
    return jax.shard_map(
        shards,
        mesh=mesh,
        in_specs=placed,
        out_specs=(P(("patch", "sub"), None), P(), P(("patch", "sub"), None), P()),
        check_vma=False,
    )
```

profile of v0, /device:TPU:1, one launch (start us, length us, event | category | flops | bytes accessed | tf_op | source)
XLA Modules:
  0.0 273.8 jit_solution(14523509861601565644)
XLA Ops:
  7.3 0.9 compare_and_fusion.4
  8.1 0.7 compare_select_fusion.1
  8.9 3.0 %gather_fusion = bf16[256,512]{1,0:T(8,128)(2,1)} fusion(bf16[512,512]{1,0:T(8,128)(2,1)} %param.19, s32[1024]{0:T(1024)S(1)} %pad_clamp_fusion.3), kind=kCustom, calls=%fused_computation.2 | custom fusion | bytes 525312 | tf_op jit(solution)/shard_map/jit(_take)/gather | solution.py:90
  11.9 1.0 broadcast_select_fusion.1
  13.6 2.6 collective-permute-start
  16.2 1.3 compare_and_fusion.2
  17.6 1.2 slice_bitcast_fusion
  18.8 1.3 compare_select_fusion.2
  20.0 1.2 compare_and_fusion.3
  21.2 1.3 compare_select_fusion
  22.6 1.3 compare_and_fusion
  23.9 1.3 fusion.59
  25.8 1.8 gather_fusion.4
  27.6 1.9 gather_fusion.3
  30.8 1.5 broadcast_select_fusion.2
  32.2 2.5 fusion.46
  34.8 43.1 %all-reduce.5 = bf16[128,512]{1,0:T(8,128)(2,1)} all-reduce(f32[128,512]{1,0:T(8,128)} %fusion.46), channel_id=1, replica_groups=mesh['patch'=8,'sub'=4] {'patch','sub'}, use_global_device_ids=true, to_apply=%region_1.3 | all-reduce | flops 65536 | bytes 393216 | tf_op jit(solution)/shard_map/psum | solution.py:88
  78.6 0.7 reshape.162
  79.3 1.4 fusion.25
  80.7 1.6 add_convert_fusion
  82.3 2.0 gather_fusion.2
  84.3 0.9 broadcast_select_fusion
  86.0 0.9 constant_dynamic-update-slice_fusion.1
  87.0 0.9 constant_dynamic-update-slice_fusion
  87.9 0.9 copy-done.6
  88.8 1.6 fusion.29
  90.5 12.8 %gather_fusion.1 = f32[3072,512]{1,0:T(8,128)} fusion(f32[769,512]{1,0:T(8,128)S(1)} %concatenate.22, s32[3072]{0:T(1024)S(1)} %broadcast_clamp_fusion), kind=kCustom, calls=%fused_computation.3 | custom fusion | bytes 12595200 | tf_op jit(solution)/shard_map/jit(_take)/gather | solution.py:98
  103.4 5.1 %multiply_reduce_fusion = bf16[512,512]{1,0:T(8,128)(2,1)S(1)} fusion(f32[6,512,512]{2,1,0:T(8,128)} %bitcast.52, f32[6,512]{1,0:T(8,128)S(1)} %get-tuple-element.14, f32[512]{0:T(512)S(1)} %copy-done.16, f32[512,512]{1,0:T(8,128)} %fusion.25, pred[6,512]{1,0:T(8,128)(4,1)S(1)} %copy-done.15), kind=kLoop, calls=%fused_computation.15 | loop fusion | flops 13893632 | bytes 7881728 | tf_op jit(solution)/shard_map/reduce_sum | solution.py:100
  108.6 2.0 select_convert_fusion.1
  110.6 1.3 fusion.19
  112.0 0.8 slice-done
  112.7 0.9 copy-done.5
  113.6 1.2 slice-done.1
  114.9 3.6 %fusion.5 = bf16[512,512]{1,0:T(8,128)(2,1)S(1)} fusion(f32[6,512]{1,0:T(8,128)S(1)} %get-tuple-element.14, f32[512]{0:T(512)S(1)} %copy-done.16, f32[512,512]{1,0:T(8,128)S(1)} %copy-done.5, f32[6,512,512]{2,1,0:T(8,128)S(1)} %bitcast.55, pred[6,512]{1,0:T(8,128)(4,1)S(1)} %copy-done.15, f32[512,512]{1,0:T(8,128)S(1)} %slice.81), kind=kLoop, calls=%fused_computation.19 | loop fusion | flops 21757952 | bytes 8930304 | tf_op jit(solution)/shard_map/reduce_sum | solution.py:115
  118.9 3.5 %fusion.3 = bf16[3072,512]{1,0:T(8,128)(2,1)S(1)} fusion(f32[3072,512]{1,0:T(8,128)S(1)} %bitcast.54, f32[3072]{0:T(1024)S(1)} %mul.107, f32[512]{0:T(512)S(1)} %copy-done.16, f32[512,512]{1,0:T(8,128)S(1)} %slice.81, f32[512,512]{1,0:T(8,128)S(1)} %copy-done.5, pred[3072]{0:T(1024)(128)(4,1)S(1)} %broadcast_in_dim.94), kind=kLoop, calls=%fused_computation.13 | loop fusion | flops 20447232 | bytes 11551744 | tf_op jit(solution)/shard_map/convert_element_type | solution.py:112
  122.4 2.6 fusion.12
  125.9 1.5 pad_maximum_fusion
  127.5 1.7 fusion.69
  129.2 1.7 collective-permute-start.3
  130.9 1.2 collective-permute-start.2
  132.1 2.8 %fusion.13 = f32[512,512]{1,0:T(8,128)} fusion(bf16[512,512]{1,0:T(8,128)(2,1)S(1)} %fusion.5, bf16[512,512]{1,0:T(8,128)(2,1)} %param.35, f32[768,512]{1,0:T(8,128)S(1)} %get-tuple-element.22, f32[512,1536]{1,0:T(8,128)} %copy-done.11, bf16[1024,512]{1,0:T(8,128)(2,1)S(1)} %copy-done.9), kind=kOutput, calls=%fused_computation.31 | convolution fusion | flops 269484032 | bytes 4718592 | tf_op jit(solution)/shard_map/dot_general | solution.py:43
  135.0 1.9 collective-permute-done.2
  136.9 3.6 %scatter_custom_fusion = f32[512,512]{1,0:T(8,128)} fusion(f32[512,512]{1,0:T(8,128)} %fusion.13, s32[128]{0:T(128)} %get-tuple-element.16, bf16[128,512]{1,0:T(8,128)(2,1)S(1)} %collective-permute-done.3, bf16[]{:T(256)} %constant.85, bf16[256,512]{1,0:T(8,128)(2,1)S(1)} %slice.84, bf16[128,512]{1,0:T(8,128)(2,1)S(1)} %collective-permute-done.2), kind=kCustom, calls=%fused_computation.55 | custom fusion | flops 458752 | bytes 1573376 | tf_op jit(solution)/shard_map/scatter-add | solution.py:132
  140.6 3.6 %scatter_custom_fusion.1 = f32[512,512]{1,0:T(8,128)} fusion(f32[512,512]{1,0:T(8,128)} %scatter_custom_fusion, s32[128]{0:T(128)} %get-tuple-element.15, bf16[128,512]{1,0:T(8,128)(2,1)S(1)} %collective-permute-done.3, bf16[]{:T(256)} %constant.85, bf16[256,512]{1,0:T(8,128)(2,1)S(1)} %slice.84, bf16[128,512]{1,0:T(8,128)(2,1)S(1)} %collective-permute-done.2), kind=kCustom, calls=%fused_computation.63 | custom fusion | flops 458752 | bytes 1573376 | tf_op jit(solution)/shard_map/scatter-add | solution.py:132
  144.2 2.2 select_convert_fusion
  146.3 114.0 %all-reduce.4.cloned.1.call-done = f32[1024,512]{1,0:T(8,128)} async-done(((f32[1024,512]{1,0:T(8,128)}), f32[1024,512]{1,0:T(8,128)}) %all-reduce.4.cloned.1.call-update) | async-done | bytes 2097168 | tf_op jit(solution)/shard_map/psum | solution.py:150
  260.4 2.7 multiply_reduce_fusion.1
  263.8 3.1 %broadcast_multiply_fusion = f32[1024,512]{1,0:T(8,128)} fusion(f32[1024,512]{1,0:T(8,128)} %all-reduce.4.cloned.1.call-done, f32[]{:T(128)S(6)} %rsqrt.3), kind=kLoop, calls=%fused_computation.39 | loop fusion | flops 524288 | bytes 4194308 | tf_op jit(solution)/shard_map/mul | solution.py:152
  (63 shorter events, 4.4 us)
Async XLA Ops:
  7.2 101.3 %copy-start = (bf16[1536,512]{1,0:T(8,128)(2,1)S(1)}, bf16[1536,512]{1,0:T(8,128)(2,1)}, u32[]{:S(2)}) copy-start(bf16[1536,512]{1,0:T(8,128)(2,1)} %param.29) | copy-start | bytes 4718596
  7.2 72.1 %copy-start.3 = (bf16[512,512]{1,0:T(8,128)(2,1)S(1)}, bf16[512,512]{1,0:T(8,128)(2,1)}, u32[]{:S(2)}) copy-start(bf16[512,512]{1,0:T(8,128)(2,1)} %param.19) | copy-start | bytes 1572868
  7.2 73.5 %copy-start.2 = (bf16[128,512]{1,0:T(8,128)(2,1)S(1)}, bf16[128,512]{1,0:T(8,128)(2,1)}, u32[]{:S(2)}) copy-start(bf16[128,512]{1,0:T(8,128)(2,1)} %param.20) | copy-start | bytes 393220
  7.2 72.1 %copy-start.8 = (bf16[1024,512]{1,0:T(8,128)(2,1)S(1)}, bf16[1024,512]{1,0:T(8,128)(2,1)}, u32[]{:S(2)}) copy-start(bf16[1024,512]{1,0:T(8,128)(2,1)} %param.27) | copy-start | bytes 3145732
  7.2 253.2 %all-reduce.4.cloned.1.call-start = ((), (), s32[]{:S(2)}) async-start(), calls=%async_computation | async-start | bytes 4194304 | tf_op jit(solution)/shard_map/psum | solution.py:150
  13.6 72.4 %collective-permute-start = (bf16[128,512]{1,0:T(8,128)(2,1)}, bf16[128,512]{1,0:T(8,128)(2,1)}, u32[]{:S(2)}, u32[]{:S(2)}) collective-permute-start(bf16[128,512]{1,0:T(8,128)(2,1)} %get-tuple-element.12), channel_id=1, source_target_pairs={{0,1},{1,2},{2,3},{3,4},{4,5},{5,6},{6,7},{7,8},{8,9},{9,10},{10,1... | collective-permute-start | bytes 393224 | tf_op jit(solution)/shard_map/ppermute | solution.py:19
  16.2 70.7 %collective-permute-start.1 = (bf16[128,512]{1,0:T(8,128)(2,1)}, bf16[128,512]{1,0:T(8,128)(2,1)}, u32[]{:S(2)}, u32[]{:S(2)}) collective-permute-start(bf16[128,512]{1,0:T(8,128)(2,1)} %get-tuple-element.11), channel_id=1, source_target_pairs={{1,0},{2,1},{3,2},{4,3},{5,4},{6,5},{7,6},{8,7},{9,8},{10,9},{11,1... | collective-permute-start | bytes 393224 | tf_op jit(solution)/shard_map/ppermute | solution.py:20
  32.2 52.1 %copy-start.17 = (pred[512]{0:T(512)(128)(4,1)S(1)}, pred[512]{0:T(512)(128)(4,1)}, u32[]{:S(2)}) copy-start(pred[512]{0:T(512)(128)(4,1)} %compare_and_fusion.3) | copy-start | bytes 1540
  34.8 51.2 %copy-start.14 = (s32[6,512]{1,0:T(8,128)S(1)}, s32[6,512]{1,0:T(8,128)}, u32[]{:S(2)}) copy-start(s32[6,512]{1,0:T(8,128)} %param.21) | copy-start | bytes 36868
  34.8 51.2 %copy-start.15 = (pred[6,512]{1,0:T(8,128)(4,1)S(1)}, pred[6,512]{1,0:T(8,128)(4,1)}, u32[]{:S(2)}) copy-start(pred[6,512]{1,0:T(8,128)(4,1)} %get-tuple-element.13) | copy-start | bytes 9220
  82.3 8.2 %copy-start.1 = (bf16[128,512]{1,0:T(8,128)(2,1)}, bf16[128,512]{1,0:T(8,128)(2,1)S(1)}, u32[]{:S(2)}) copy-start(bf16[128,512]{1,0:T(8,128)(2,1)S(1)} %add_convert_fusion) | copy-start | bytes 393220
  87.9 0.9 copy-start.6
  90.5 12.9 %copy-start.16 = (f32[512]{0:T(512)S(1)}, f32[512]{0:T(512)}, u32[]{:S(2)}) copy-start(f32[512]{0:T(512)} %param.28) | copy-start | bytes 6148
  103.4 5.2 %copy-start.4 = (bf16[512,512]{1,0:T(8,128)(2,1)S(1)}, bf16[512,512]{1,0:T(8,128)(2,1)}, u32[]{:S(2)}) copy-start(bf16[512,512]{1,0:T(8,128)(2,1)} %param.19) | copy-start | bytes 1572868
  103.4 5.2 %copy-start.13 = (bf16[512,512]{1,0:T(8,128)(2,1)S(1)}, bf16[512,512]{1,0:T(8,128)(2,1)}, u32[]{:S(2)}) copy-start(bf16[512,512]{1,0:T(8,128)(2,1)} %broadcast_select_fusion) | copy-start | bytes 1572868
  103.4 5.2 %copy-start.18 = (f32[512]{0:T(512)S(1)}, f32[512]{0:T(512)}, u32[]{:S(2)}) copy-start(f32[512]{0:T(512)} %param.30) | copy-start | bytes 6148
  108.5 2.0 copy-start.12
  110.6 2.2 slice-start
  110.6 3.1 %copy-start.5 = (f32[512,512]{1,0:T(8,128)S(1)}, f32[512,512]{1,0:T(8,128)}, u32[]{:S(2)}) copy-start(f32[512,512]{1,0:T(8,128)} %fusion.25) | copy-start | bytes 3145732
  110.6 4.3 %slice-start.1 = ((s8[6291456]{0:T(1024)(128)(4,1)}), s8[2097152]{0:T(1024)(128)(4,1)S(1)}, s32[]{:S(2)}) async-start(s8[6291456]{0:T(1024)(128)(4,1)} %bitcast.53), calls=%async_computation.2 | async-start | bytes 4194304
  111.9 6.6 %copy-start.11 = (f32[512,1536]{1,0:T(8,128)}, f32[512,1536]{1,0:T(8,128)S(1)}, u32[]{:S(2)}) copy-start(f32[512,1536]{1,0:T(8,128)S(1)} %fusion.19) | copy-start | bytes 9437188
  122.4 2.6 copy-start.7
  125.0 0.9 copy-start.10
  125.0 2.4 copy-start.9
  129.2 5.8 %collective-permute-start.3 = (bf16[128,512]{1,0:T(8,128)(2,1)S(1)}, bf16[128,512]{1,0:T(8,128)(2,1)S(1)}, u32[]{:S(2)}, u32[]{:S(2)}) collective-permute-start(bf16[128,512]{1,0:T(8,128)(2,1)S(1)} %get-tuple-element.10), channel_id=1, source_target_pairs={{1,0},{2,1},{3,2},{4,3},{5,4},{6,5},{7,6},{8,7},{9,8},{10,9},{11,1... | collective-permute-start | bytes 393224 | tf_op jit(solution)/shard_map/ppermute | solution.py:20
  130.9 6.0 %collective-permute-start.2 = (bf16[128,512]{1,0:T(8,128)(2,1)S(1)}, bf16[128,512]{1,0:T(8,128)(2,1)S(1)}, u32[]{:S(2)}, u32[]{:S(2)}) collective-permute-start(bf16[128,512]{1,0:T(8,128)(2,1)S(1)} %get-tuple-element.9), channel_id=1, source_target_pairs={{0,1},{1,2},{2,3},{3,4},{4,5},{5,6},{6,7},{7,8},{8,9},{9,10},{10,1... | collective-permute-start | bytes 393224 | tf_op jit(solution)/shard_map/ppermute | solution.py:19
Sparse Core Ops, SparseCore 0:
  127.6 132.7 all-reduce.3
where the time goes:
time: 277 us; the launch traced here: 274 us
  waiting for transfers between devices  116 us (42%)
  other arithmetic  43.6 us (16%)
  blocking collectives  43.1 us (16%)
  local copies, waits for them, and re-layouts  30.4 us (11%)
  matrix products  18.7 us (7%)
  between operations  16.4 us (6%)
  starting transfers between devices  5.54 us (2%)
    psum x1, waiting for transfers between devices, shards(): raw_grad = lax.psum(partial_grad, ('patch', 'sub'))  114 us
    psum x1, blocking collectives, shards(): summed = lax.psum(partial_sum, ('patch', 'sub')).astype(jnp.bfloat16)  43.1 us
    gather x1, local copies, waits for them, and re-layouts, shards(): jnp.take(source_proj, neighbours, axis=0) + target_proj[None] + msg_bias  12.8 us
    scatter-add x2, other arithmetic, shards(): returned.at[send_rows[0, 0]].add(from_prev_grad).at[send_rows[0, 1]]  7.24 us
    dot_general x3, matrix products, transposed_product(): lax.dot_general(left, right, (((1,), (1,)), ((), ())), preferred_element_...  5.88 us
  transfers between devices with their start and end apart: 5, of which 2 were waited for; matrix products, arithmetic and copies ran while one was open for 15% of the time, Pallas kernels for 0%

commit v1 on v0

v1 whole, which is shorter than its diff:
```python
import functools

import jax
import jax.numpy as jnp
from jax import lax
from jax.experimental import pallas as pl
from jax.experimental.pallas import tpu as pltpu
from jax.sharding import PartitionSpec as P

MESH = pl.DeviceIdType.MESH
AXES = ("patch", "sub")
epsilon = 1e-06
BF = jnp.bfloat16
F32 = jnp.float32


def mm(a, b):
    return jnp.dot(a, b, preferred_element_type=F32)


def mm_nt(a, b):
    return lax.dot_general(a, b, (((1,), (1,)), ((), ())), preferred_element_type=F32)


def mm_tn(a, b):
    return lax.dot_general(a, b, (((0,), (0,)), ((), ())), preferred_element_type=F32)


def sigmoid(v):
    return 0.5 + 0.5 * jnp.tanh(0.5 * v)


def onehot_rows(count, row):
    at = lax.broadcasted_iota(jnp.int32, (count, row.shape[1]), 0)
    return jnp.where(at == row, 1.0, 0.0).astype(BF)


def layer_kernel(
    patches, subs, cut,
    real_ref, live_ref, nb_ref, send_ref, parent_ref, edges_ref, coarse_ref,
    mbias_ref, nbias_ref, cmbias_ref, cnbias_ref,
    fine_hbm, msgw_hbm, nodew_hbm, cmw_hbm, cnw_hbm, og_hbm,
    newfine_ref, newcoarse_ref, nodegrad_ref, raw_hbm, factor_ref,
    lookup, msgw, nodew, cmw, cnw, og, load_sem,
    outgoing, ret, retout, halo_ssem, halo_rsem,
    cbuf, crecv, cag, c_sem,
    pick, slopes, edelta, source, tdelta, dsum, local, sends_oh,
    gbuf, recv_a, sum_b, recv_b, ag, g_sem, out_sem,
):
    n = patches * subs
    half = n // 2
    rows, width = og.shape
    send = outgoing.shape[1]
    table = lookup.shape[0]
    deg = nb_ref.shape[0]
    cn = coarse_ref.shape[0]
    _, _, rpc, cpc = gbuf.shape
    crow, ccol = cbuf.shape[1:]
    me = lax.axis_index("patch") * subs + lax.axis_index("sub")
    par = lax.rem(me, 2)
    group = lax.div(me, 2)

    def dev(i):
        return (lax.div(i, subs), lax.rem(i, subs))

    partner = dev(me + 1 - 2 * par)
    nxt, prv = dev(lax.rem(me + 1, n)), dev(lax.rem(me + n - 1, n))

    def remote(src, dst, ssem, rsem, to):
        return pltpu.make_async_remote_copy(
            src_ref=src, dst_ref=dst, send_sem=ssem, recv_sem=rsem,
            device_id=to, device_id_type=MESH,
        )

    barrier = pltpu.get_barrier_semaphore()

    def greet(o, c):
        pl.semaphore_signal(barrier, inc=1, device_id=dev(lax.rem(me + o, n)), device_id_type=MESH)
        return c

    loads = [
        pltpu.make_async_copy(fine_hbm, lookup.at[pl.ds(0, rows)], load_sem.at[0]),
        pltpu.make_async_copy(cmw_hbm, cmw, load_sem.at[1]),
        pltpu.make_async_copy(msgw_hbm, msgw, load_sem.at[2]),
        pltpu.make_async_copy(nodew_hbm, nodew, load_sem.at[3]),
        pltpu.make_async_copy(cnw_hbm, cnw, load_sem.at[4]),
        pltpu.make_async_copy(og_hbm, og, load_sem.at[5]),
    ]
    for load in loads:
        load.start()
    lax.fori_loop(1, n, greet, 0)

    sends_oh[:, :send] = onehot_rows(rows, send_ref[0:1, :])
    sends_oh[:, send:] = onehot_rows(rows, send_ref[1:2, :])
    loads[0].wait()
    fine = lookup[pl.ds(0, rows), :]
    gathered = mm_tn(sends_oh[...], fine).astype(BF)
    outgoing[0] = gathered[:send]
    outgoing[1] = gathered[send:]
    pl.semaphore_wait(barrier, n - 1)
    halo = [
        remote(outgoing.at[1], lookup.at[pl.ds(rows, send)], halo_ssem.at[0], halo_rsem.at[0], nxt),
        remote(outgoing.at[0], lookup.at[pl.ds(rows + send, send)], halo_ssem.at[1], halo_rsem.at[1], prv),
    ]
    for copy in halo:
        copy.start()

    coarse = coarse_ref[...]
    to_sender = onehot_rows(cn, edges_ref[0:1, :])
    to_receiver = onehot_rows(cn, edges_ref[1:2, :])
    senders = mm_tn(to_sender, coarse).astype(BF)
    receivers = mm_tn(to_receiver, coarse).astype(BF)
    loads[1].wait()
    pre = mm(senders, cmw[:width, :]) + mm(receivers, cmw[width:, :]) + cmbias_ref[...]
    slot = lax.broadcasted_iota(jnp.int32, pre.shape, 0)
    message = jnp.where(slot < live_ref[0], pre * sigmoid(pre), 0.0).astype(BF)
    partial = mm(to_receiver, message).astype(BF)
    blocks = cn // crow
    for cb in range(width // ccol):
        cbuf[pl.ds(cb * blocks, blocks)] = partial[:, cb * ccol:(cb + 1) * ccol].reshape(blocks, crow, ccol)

    def send_partial(o, c):
        to = lax.rem(me + o, n)
        remote(cbuf.at[to], crecv.at[o - 1], c_sem.at[0], c_sem.at[1], dev(to)).start()
        return c

    lax.fori_loop(1, n, send_partial, 0)

    loads[2].wait()
    source[pl.ds(0, rows), :] = mm(fine, msgw[:width, :]).astype(BF)
    target = mm(fine, msgw[width:, :]) + mbias_ref[...]
    local[...] = target
    for k in range(deg):
        pick[:, k * rows:(k + 1) * rows] = onehot_rows(table, nb_ref[k:k + 1, :])

    remote(crecv, crecv, c_sem.at[0], c_sem.at[1], partner).wait_recv()
    share = jnp.sum(crecv[...].astype(F32), axis=0) + cbuf[me].astype(F32)
    cag[me] = share.astype(BF)

    def send_share(o, c):
        remote(cag.at[me], cag.at[me], c_sem.at[2], c_sem.at[3], dev(lax.rem(me + o, n))).start()
        return c

    lax.fori_loop(1, n, send_share, 0)

    for copy in halo:
        copy.wait_recv()
    source[pl.ds(rows, table - rows), :] = mm(lookup[pl.ds(rows, table - rows), :], msgw[:width, :]).astype(BF)
    nb = jnp.concatenate([nb_ref[...], nb_ref[0:8 - deg, :]], 0)
    nb_col = nb.astype(F32).T.astype(jnp.int32)
    tile = rows // 2
    parts = []
    for t in range(2):
        agg = jnp.zeros((tile, width), F32)
        tgt = local[pl.ds(t * tile, tile), :]
        at = lax.broadcasted_iota(jnp.int32, (tile, table), 1)
        for k in range(deg):
            col = nb_col[t * tile:(t + 1) * tile, k:k + 1]
            hot = jnp.where(at == col, 1.0, 0.0).astype(BF)
            v = mm(hot, source[...]) + tgt
            filled = jnp.where(col < table, 1.0, 0.0)
            s = sigmoid(v) * filled
            silu = v * s
            agg = agg + silu
            slopes[k, pl.ds(t * tile, tile), :] = s + silu * (1.0 - s)
        parts.append(agg.astype(BF))
    aggregated = jnp.concatenate(parts, 0)

    loads[3].wait()
    first = mm(fine, nodew[:width, :]) + mm(aggregated, nodew[width:2 * width, :]) + nbias_ref[...]
    loads[4].wait()
    remote(crecv, crecv, c_sem.at[2], c_sem.at[3], partner).wait_recv()
    summed = jnp.concatenate(
        [cag[pl.ds(cb * blocks, blocks)].reshape(cn, ccol) for cb in range(width // ccol)], 1
    )
    hidden = mm(coarse, cnw[:width, :]) + mm(summed, cnw[width:, :]) + cnbias_ref[...]
    new_coarse = (coarse.astype(F32) + hidden * sigmoid(hidden)).astype(BF)
    newcoarse_ref[...] = new_coarse

    lifted = mm_tn(onehot_rows(cn, parent_ref[...]), new_coarse).astype(BF)
    node_pre = first + mm(lifted, nodew[2 * width:, :])
    real = lax.broadcasted_iota(jnp.int32, (rows, width), 0) < real_ref[0]
    s = sigmoid(node_pre)
    silu = node_pre * s
    newfine_ref[...] = jnp.where(real, fine.astype(F32) + silu, 0.0).astype(BF)
    loads[5].wait()
    out_grad = og[...].astype(F32)
    node_delta = jnp.where(real, out_grad * (s + silu * (1.0 - s)), 0.0).astype(BF)
    back = mm_nt(node_delta, nodew[width:2 * width, :])
    total = jnp.zeros((rows, width), F32)
    for k in range(deg):
        ed = (back * slopes[k]).astype(BF)
        edelta[pl.ds(k * rows, rows), :] = ed
        total = total + ed.astype(F32)
    dsum[...] = total.astype(BF)

    tdelta[pl.ds(rows, table - rows), :] = mm(pick[pl.ds(rows, table - rows), :], edelta[...]).astype(BF)
    rim = mm_nt(tdelta[pl.ds(rows, table - rows), :], msgw[:width, :]).astype(BF)
    retout[0] = rim[:send]
    retout[1] = rim[send:]
    give = [
        remote(retout.at[1], ret.at[0], halo_ssem.at[2], halo_rsem.at[2], nxt),
        remote(retout.at[0], ret.at[1], halo_ssem.at[3], halo_rsem.at[3], prv),
    ]
    for copy in give:
        copy.start()
    tdelta[pl.ds(0, rows), :] = mm(pick[pl.ds(0, rows), :], edelta[...]).astype(BF)

    def keep(grad, base):
        for i in range(grad.shape[0] // rpc):
            for j in range(cut):
                c = (base // rpc + i) * cut + j
                gbuf[c % 2, c // 2] = grad[i * rpc:(i + 1) * rpc, j * cpc:(j + 1) * cpc]

    keep(mm_tn(lookup[...], tdelta[...]).astype(BF), 0)
    keep(mm_tn(fine, dsum[...]).astype(BF), width)
    swap = remote(gbuf.at[1 - par], recv_a, g_sem.at[0], g_sem.at[1], partner)
    swap.start()
    local[...] = out_grad + mm_nt(node_delta, nodew[:width, :])
    swap.wait_recv()
    sum_b[...] = (gbuf[par].astype(F32) + recv_a[...].astype(F32)).astype(BF)

    def send_chunk(o, c):
        to = lax.rem(group + o, half)
        remote(sum_b.at[to], recv_b.at[o - 1], g_sem.at[2], g_sem.at[3], dev(2 * to + par)).start()
        return c

    lax.fori_loop(1, half, send_chunk, 0)

    grad = local[...] + mm_nt(dsum[...], msgw[width:, :]) + mm_nt(tdelta[pl.ds(0, rows), :], msgw[:width, :])
    for copy in give:
        copy.wait_recv()
    grad = grad + mm(sends_oh[:, :send], ret[0]) + mm(sends_oh[:, send:], ret[1])
    nodegrad_ref[...] = jnp.where(real, grad, 0.0).astype(BF)

    remote(recv_b, recv_b, g_sem.at[2], g_sem.at[3], partner).wait_recv()
    chunk = jnp.sum(recv_b[...].astype(F32), axis=0) + sum_b[group].astype(F32)
    ag[par, group] = chunk.astype(BF)

    def send_sum(o, c):
        to = lax.rem(group + o, half)
        mine = ag.at[par, group]
        remote(mine, mine, g_sem.at[4], g_sem.at[5], dev(2 * to + par)).start()
        return c

    lax.fori_loop(1, half, send_sum, 0)
    remote(recv_b, recv_b, g_sem.at[4], g_sem.at[5], partner).wait_recv()
    last = remote(ag.at[par], ag.at[par], g_sem.at[6], g_sem.at[7], partner)
    last.start()
    last.wait_recv()
    out = pltpu.make_async_copy(ag, raw_hbm, out_sem)
    out.start()
    raw = ag[...].astype(F32)
    mean = jnp.sum(raw * raw) / (2 * width * width)
    factor_ref[...] = jnp.full(factor_ref.shape, lax.rsqrt(mean + epsilon), F32)

    for copy in halo + give:
        copy.wait_send()
    remote(crecv, crecv, c_sem.at[0], c_sem.at[1], partner).wait_send()
    remote(crecv, crecv, c_sem.at[2], c_sem.at[3], partner).wait_send()
    swap.wait_send()
    remote(recv_b, recv_b, g_sem.at[2], g_sem.at[3], partner).wait_send()
    remote(recv_b, recv_b, g_sem.at[4], g_sem.at[5], partner).wait_send()
    last.wait_send()
    out.wait()


def shards(
    patches, subs,
    fine_nodes, coarse_nodes, neighbours, send_rows, real_rows, parent,
    coarse_edges, coarse_live, msg_weight, msg_bias, node_weight, node_bias,
    coarse_msg_weight, coarse_msg_bias, coarse_node_weight, coarse_node_bias,
    out_grad,
):
    n = patches * subs
    half = n // 2
    rows, width = fine_nodes.shape
    send = send_rows.shape[2]
    table = rows + 2 * send
    deg = neighbours.shape[0]
    cn = coarse_nodes.shape[0]
    cut = max(1, 16 * n // (2 * width))
    rpc, cpc = 2 * width * cut // n, width // cut
    ccol = 128
    crow = cn * (width // ccol) // n
    vmem = pl.BlockSpec(memory_space=pltpu.VMEM)
    smem = pl.BlockSpec(memory_space=pltpu.SMEM)
    hbm = pl.BlockSpec(memory_space=pl.ANY)
    V = pltpu.VMEM
    dma = pltpu.SemaphoreType.DMA
    new_fine, new_coarse, node_grad, raw, factor = pl.pallas_call(
        functools.partial(layer_kernel, patches, subs, cut),
        out_shape=(
            jax.ShapeDtypeStruct((rows, width), BF),
            jax.ShapeDtypeStruct((cn, width), BF),
            jax.ShapeDtypeStruct((rows, width), BF),
            jax.ShapeDtypeStruct((2, half, rpc, cpc), BF),
            jax.ShapeDtypeStruct((8, 128), F32),
        ),
        in_specs=[smem, smem] + [vmem] * 9 + [hbm] * 6,
        out_specs=(vmem, vmem, vmem, hbm, vmem),
        scratch_shapes=[
            V((table, width), BF), V((2 * width, width), BF), V((3 * width, width), BF),
            V((2 * width, width), BF), V((2 * width, width), BF), V((rows, width), BF), dma((6,)),
            V((2, send, width), BF), V((2, send, width), BF), V((2, send, width), BF), dma((4,)), dma((4,)),
            V((n, crow, ccol), BF), V((n - 1, crow, ccol), BF), V((n, crow, ccol), BF), dma((4,)),
            V((table, deg * rows), BF), V((deg, rows, width), F32), V((deg * rows, width), BF),
            V((table, width), BF), V((table, width), BF), V((rows, width), BF),
            V((rows, width), F32), V((rows, 2 * send), BF),
            V((2, half, rpc, cpc), BF), V((half, rpc, cpc), BF), V((half, rpc, cpc), BF),
            V((half - 1, rpc, cpc), BF), V((2, half, rpc, cpc), BF), dma((8,)), dma,
        ],
        compiler_params=pltpu.CompilerParams(
            collective_id=0, has_side_effects=True, vmem_limit_bytes=56 * 1024 * 1024
        ),
        name="layer",
    )(
        real_rows, coarse_live, neighbours, send_rows[0], parent[None, :], coarse_edges, coarse_nodes,
        msg_bias[None, :], node_bias[None, :], coarse_msg_bias[None, :], coarse_node_bias[None, :],
        fine_nodes, msg_weight, node_weight, coarse_msg_weight, coarse_node_weight, out_grad,
    )
    ordered = raw.transpose(1, 0, 2, 3).reshape(2 * width // rpc, cut, rpc, cpc).transpose(0, 2, 1, 3)
    msg_weight_grad = ordered.reshape(2 * width, width).astype(F32) * factor[0, 0]
    return new_fine, new_coarse, node_grad, msg_weight_grad


def solution(mesh):
    both = P(AXES)
    placed = (
        P(AXES, None), P(), P(None, AXES), P(AXES, None, None), both, both, P(None, AXES), both,
        P(), P(), P(), P(), P(), P(), P(), P(), P(AXES, None),
    )
    return jax.shard_map(
        functools.partial(shards, mesh.shape["patch"], mesh.shape["sub"]),
        mesh=mesh,
        in_specs=placed,
        out_specs=(P(AXES, None), P(), P(AXES, None), P()),
        check_vma=False,
    )
```

time: 277 us -> 65.6 us (0.24)
  the two profiles are of different devices: /device:TPU:1 before, /device:TPU:29 now
where the time goes in v1:
time: 65.6 us; the launch traced here: 65.4 us
  Pallas kernels  56.3 us (86%)
  local copies, waits for them, and re-layouts  4.96 us (8%)
  other arithmetic  2.15 us (3%)
  between operations  1.97 us (3%)
    pallas_call x1, Pallas kernels, shards(): pl.pallas_call(functools.partial(layer_kernel, patches, subs, cut), out_s...  56.3 us
    unnamed x9, local copies, waits for them, and re-layouts  2.25 us
    mul x1, other arithmetic, shards(): ordered.reshape(2 * width, width).astype(F32) * factor[0, 0]  2.15 us
    mul x1, local copies, waits for them, and re-layouts, shards(): ordered.reshape(2 * width, width).astype(F32) * factor[0, 0]  1.52 us

profile of v1, /device:TPU:29, one launch (start us, length us, event | category | flops | bytes accessed | tf_op | source)
XLA Modules:
  0.0 65.4 jit_solution(2473895014206122779)
XLA Ops:
  1.9 56.3 %layer.1 = (bf16[512,512]{1,0:T(8,128)(2,1)}, bf16[128,512]{1,0:T(8,128)(2,1)}, bf16[512,512]{1,0:T(8,128)(2,1)}, bf16[2,16,32,512]{3,2,1,0:T(8,128)(2,1)}, f32[8,128]{1,0:T(8,128)}) custom-call(s32[1]{0:T(128)S(6)} %copy.25.real_ref, s32[1]{0:T(128)S(6)} %copy.26.live_ref, s32[6,512]{1,0:T(8,128)} %nb_ref.1, s32[2,128]{1,0:T(2,128)} %bitcast.16, ...), custom_call_target="tpu_custom_call" | custom-call | tf_op jit(solution)/shard_map/layer/pallas_call | solution.py:291
  58.3 1.2 %slice.3 = f32[1,1]{1,0:T(1,128)} slice(f32[8,128]{1,0:T(8,128)} %get-tuple-element.13), slice={[0:1], [0:1]} | slice | bytes 8 | tf_op jit(solution)/shard_map/slice | solution.py:323
  59.4 2.1 %multiply_bitcast_fusion = f32[16,2,32,512]{3,2,0,1:T(8,128)S(1)} fusion(bf16[2,16,32,512]{3,2,1,0:T(8,128)(2,1)} %get-tuple-element.12, f32[]{:T(128)} %bitcast.6), kind=kLoop, calls=%fused_computation | loop fusion | flops 1048576 | bytes 3145732 | tf_op jit(solution)/shard_map/mul | solution.py:323
  61.6 0.0 copy-start.1
  61.6 0.0 copy-start.2
  61.6 0.0 copy-start
  61.6 1.5 %copy.21 = f32[16,2,32,512]{3,2,1,0:T(8,128)} copy(f32[16,2,32,512]{3,2,0,1:T(8,128)S(1)} %multiply_bitcast_fusion) | data formatting | bytes 4194304 | tf_op jit(solution)/shard_map/mul | solution.py:323
  63.1 0.0 copy-done.1
  63.2 0.8 %copy.27 = bf16[512,512]{1,0:T(8,128)(2,1)} copy(bf16[512,512]{1,0:T(8,128)(2,1)S(1)} %copy-done.1) | data formatting | bytes 1048576
  63.9 0.0 copy-done.2
  63.9 0.7 %copy.28 = bf16[128,512]{1,0:T(8,128)(2,1)} copy(bf16[128,512]{1,0:T(8,128)(2,1)S(1)} %copy-done.2) | data formatting | bytes 262144
  64.6 0.0 copy-done
  64.6 0.8 %copy.29 = bf16[512,512]{1,0:T(8,128)(2,1)} copy(bf16[512,512]{1,0:T(8,128)(2,1)S(1)} %copy-done) | data formatting | bytes 1048576
Async XLA Ops:
  61.6 1.6 %copy-start.1 = (bf16[512,512]{1,0:T(8,128)(2,1)S(1)}, bf16[512,512]{1,0:T(8,128)(2,1)}, u32[]{:S(2)}) copy-start(bf16[512,512]{1,0:T(8,128)(2,1)} %get-tuple-element.18) | copy-start | bytes 1572868
  61.6 2.3 %copy-start.2 = (bf16[128,512]{1,0:T(8,128)(2,1)S(1)}, bf16[128,512]{1,0:T(8,128)(2,1)}, u32[]{:S(2)}) copy-start(bf16[128,512]{1,0:T(8,128)(2,1)} %get-tuple-element.19) | copy-start | bytes 393220
  61.6 3.0 %copy-start = (bf16[512,512]{1,0:T(8,128)(2,1)S(1)}, bf16[512,512]{1,0:T(8,128)(2,1)}, u32[]{:S(2)}) copy-start(bf16[512,512]{1,0:T(8,128)(2,1)} %get-tuple-element.20) | copy-start | bytes 1572868

commit v2 on v1

--- a/solution.py
+++ b/solution.py
@@ -45,7 +45,7 @@
     outgoing, ret, retout, halo_ssem, halo_rsem,
     cbuf, crecv, cag, c_sem,
     pick, slopes, edelta, source, tdelta, dsum, local, sends_oh,
-    gbuf, recv_a, sum_b, recv_b, ag, g_sem, out_sem,
+    gbuf, recv_a, sum_b, recv_b, ag, g_sem, ag_sem, out_sem,
 ):
     n = patches * subs
     half = n // 2
@@ -97,14 +97,6 @@
     gathered = mm_tn(sends_oh[...], fine).astype(BF)
     outgoing[0] = gathered[:send]
     outgoing[1] = gathered[send:]
-    pl.semaphore_wait(barrier, n - 1)
-    halo = [
-        remote(outgoing.at[1], lookup.at[pl.ds(rows, send)], halo_ssem.at[0], halo_rsem.at[0], nxt),
-        remote(outgoing.at[0], lookup.at[pl.ds(rows + send, send)], halo_ssem.at[1], halo_rsem.at[1], prv),
-    ]
-    for copy in halo:
-        copy.start()
-
     coarse = coarse_ref[...]
     to_sender = onehot_rows(cn, edges_ref[0:1, :])
     to_receiver = onehot_rows(cn, edges_ref[1:2, :])
@@ -119,6 +111,14 @@
     for cb in range(width // ccol):
         cbuf[pl.ds(cb * blocks, blocks)] = partial[:, cb * ccol:(cb + 1) * ccol].reshape(blocks, crow, ccol)
 
+    pl.semaphore_wait(barrier, n - 1)
+    halo = [
+        remote(outgoing.at[1], lookup.at[pl.ds(rows, send)], halo_ssem.at[0], halo_rsem.at[0], nxt),
+        remote(outgoing.at[0], lookup.at[pl.ds(rows + send, send)], halo_ssem.at[1], halo_rsem.at[1], prv),
+    ]
+    for copy in halo:
+        copy.start()
+
     def send_partial(o, c):
         to = lax.rem(me + o, n)
         remote(cbuf.at[to], crecv.at[o - 1], c_sem.at[0], c_sem.at[1], dev(to)).start()
@@ -133,16 +133,8 @@
     for k in range(deg):
         pick[:, k * rows:(k + 1) * rows] = onehot_rows(table, nb_ref[k:k + 1, :])
 
-    remote(crecv, crecv, c_sem.at[0], c_sem.at[1], partner).wait_recv()
-    share = jnp.sum(crecv[...].astype(F32), axis=0) + cbuf[me].astype(F32)
-    cag[me] = share.astype(BF)
-
-    def send_share(o, c):
-        remote(cag.at[me], cag.at[me], c_sem.at[2], c_sem.at[3], dev(lax.rem(me + o, n))).start()
-        return c
-
-    lax.fori_loop(1, n, send_share, 0)
-
+    loads[3].wait()
+    first = mm(fine, nodew[:width, :]) + nbias_ref[...]
     for copy in halo:
         copy.wait_recv()
     source[pl.ds(rows, table - rows), :] = mm(lookup[pl.ds(rows, table - rows), :], msgw[:width, :]).astype(BF)
@@ -164,10 +156,19 @@
             agg = agg + silu
             slopes[k, pl.ds(t * tile, tile), :] = s + silu * (1.0 - s)
         parts.append(agg.astype(BF))
+        if t == 0:
+            remote(crecv, crecv, c_sem.at[0], c_sem.at[1], partner).wait_recv()
+            share = jnp.sum(crecv[...].astype(F32), axis=0) + cbuf[me].astype(F32)
+            cag[me] = share.astype(BF)
+
+            def send_share(o, c):
+                remote(cag.at[me], cag.at[me], c_sem.at[2], c_sem.at[3], dev(lax.rem(me + o, n))).start()
+                return c
+
+            lax.fori_loop(1, n, send_share, 0)
     aggregated = jnp.concatenate(parts, 0)
 
-    loads[3].wait()
-    first = mm(fine, nodew[:width, :]) + mm(aggregated, nodew[width:2 * width, :]) + nbias_ref[...]
+    first = first + mm(aggregated, nodew[width:2 * width, :])
     loads[4].wait()
     remote(crecv, crecv, c_sem.at[2], c_sem.at[3], partner).wait_recv()
     summed = jnp.concatenate(
@@ -194,6 +195,54 @@
         total = total + ed.astype(F32)
     dsum[...] = total.astype(BF)
 
+    def keep(grad, which):
+        for i in range(width // rpc):
+            for j in range(cut):
+                gbuf[which, i * cut + j] = grad[i * rpc:(i + 1) * rpc, j * cpc:(j + 1) * cpc]
+
+    swap = remote(gbuf.at[1 - par], recv_a, g_sem.at[0], g_sem.at[1], partner)
+
+    def scatter(which):
+        swap.wait_recv()
+        sum_b[...] = (gbuf[which].astype(F32) + recv_a[...].astype(F32)).astype(BF)
+
+        def send_chunk(o, c):
+            to = lax.rem(group + o, half)
+            remote(sum_b.at[to], recv_b.at[o - 1], g_sem.at[2], g_sem.at[3], dev(2 * to + par)).start()
+            return c
+
+        lax.fori_loop(1, half, send_chunk, 0)
+
+    def reduce(which):
+        remote(recv_b, recv_b, g_sem.at[2], g_sem.at[3], partner).wait_recv()
+        chunk = jnp.sum(recv_b[...].astype(F32), axis=0) + sum_b[group].astype(F32)
+        ag[which, group] = chunk.astype(BF)
+        mine = ag.at[which, group]
+        remote(mine, mine, g_sem.at[5], g_sem.at[6], partner).start()
+
+        def send_sum(o, c):
+            to = lax.rem(group + o, half)
+            remote(mine, mine, g_sem.at[4], ag_sem.at[o], dev(2 * to + par)).start()
+            return c
+
+        lax.fori_loop(1, half, send_sum, 0)
+
+    def forward(which):
+        def pass_on(o, c):
+            got = ag.at[which, lax.rem(group + half - o, half)]
+            remote(got, got, g_sem.at[4], ag_sem.at[o], partner).wait_recv()
+            remote(got, got, g_sem.at[5], g_sem.at[6], partner).start()
+            return c
+
+        lax.fori_loop(1, half, pass_on, 0)
+
+    odd, even = par == 1, par == 0
+    keep(mm_tn(fine, dsum[...]).astype(BF), 1)
+
+    @pl.when(even)
+    def _():
+        swap.start()
+
     tdelta[pl.ds(rows, table - rows), :] = mm(pick[pl.ds(rows, table - rows), :], edelta[...]).astype(BF)
     rim = mm_nt(tdelta[pl.ds(rows, table - rows), :], msgw[:width, :]).astype(BF)
     retout[0] = rim[:send]
@@ -204,28 +253,27 @@
     ]
     for copy in give:
         copy.start()
+
+    @pl.when(odd)
+    def _():
+        scatter(1)
+
     tdelta[pl.ds(0, rows), :] = mm(pick[pl.ds(0, rows), :], edelta[...]).astype(BF)
-
-    def keep(grad, base):
-        for i in range(grad.shape[0] // rpc):
-            for j in range(cut):
-                c = (base // rpc + i) * cut + j
-                gbuf[c % 2, c // 2] = grad[i * rpc:(i + 1) * rpc, j * cpc:(j + 1) * cpc]
-
     keep(mm_tn(lookup[...], tdelta[...]).astype(BF), 0)
-    keep(mm_tn(fine, dsum[...]).astype(BF), width)
-    swap = remote(gbuf.at[1 - par], recv_a, g_sem.at[0], g_sem.at[1], partner)
-    swap.start()
+
+    @pl.when(odd)
+    def _():
+        swap.start()
+
     local[...] = out_grad + mm_nt(node_delta, nodew[:width, :])
-    swap.wait_recv()
-    sum_b[...] = (gbuf[par].astype(F32) + recv_a[...].astype(F32)).astype(BF)
-
-    def send_chunk(o, c):
-        to = lax.rem(group + o, half)
-        remote(sum_b.at[to], recv_b.at[o - 1], g_sem.at[2], g_sem.at[3], dev(2 * to + par)).start()
-        return c
-
-    lax.fori_loop(1, half, send_chunk, 0)
+
+    @pl.when(even)
+    def _():
+        scatter(0)
+
+    @pl.when(odd)
+    def _():
+        reduce(1)
 
     grad = local[...] + mm_nt(dsum[...], msgw[width:, :]) + mm_nt(tdelta[pl.ds(0, rows), :], msgw[:width, :])
     for copy in give:
@@ -233,21 +281,17 @@
     grad = grad + mm(sends_oh[:, :send], ret[0]) + mm(sends_oh[:, send:], ret[1])
     nodegrad_ref[...] = jnp.where(real, grad, 0.0).astype(BF)
 
-    remote(recv_b, recv_b, g_sem.at[2], g_sem.at[3], partner).wait_recv()
-    chunk = jnp.sum(recv_b[...].astype(F32), axis=0) + sum_b[group].astype(F32)
-    ag[par, group] = chunk.astype(BF)
-
-    def send_sum(o, c):
-        to = lax.rem(group + o, half)
-        mine = ag.at[par, group]
-        remote(mine, mine, g_sem.at[4], g_sem.at[5], dev(2 * to + par)).start()
-        return c
-
-    lax.fori_loop(1, half, send_sum, 0)
-    remote(recv_b, recv_b, g_sem.at[4], g_sem.at[5], partner).wait_recv()
-    last = remote(ag.at[par], ag.at[par], g_sem.at[6], g_sem.at[7], partner)
-    last.start()
-    last.wait_recv()
+    @pl.when(even)
+    def _():
+        reduce(0)
+        forward(0)
+
+    @pl.when(odd)
+    def _():
+        forward(1)
+
+    whole_half = remote(recv_a, recv_a, g_sem.at[5], g_sem.at[6], partner)
+    whole_half.wait_recv()
     out = pltpu.make_async_copy(ag, raw_hbm, out_sem)
     out.start()
     raw = ag[...].astype(F32)
@@ -260,8 +304,8 @@
     remote(crecv, crecv, c_sem.at[2], c_sem.at[3], partner).wait_send()
     swap.wait_send()
     remote(recv_b, recv_b, g_sem.at[2], g_sem.at[3], partner).wait_send()
-    remote(recv_b, recv_b, g_sem.at[4], g_sem.at[5], partner).wait_send()
-    last.wait_send()
+    remote(recv_b, recv_b, g_sem.at[4], g_sem.at[3], partner).wait_send()
+    whole_half.wait_send()
     out.wait()
 
 
@@ -295,7 +339,7 @@
             jax.ShapeDtypeStruct((cn, width), BF),
             jax.ShapeDtypeStruct((rows, width), BF),
             jax.ShapeDtypeStruct((2, half, rpc, cpc), BF),
-            jax.ShapeDtypeStruct((8, 128), F32),
+            jax.ShapeDtypeStruct((1, width), F32),
         ),
         in_specs=[smem, smem] + [vmem] * 9 + [hbm] * 6,
         out_specs=(vmem, vmem, vmem, hbm, vmem),
@@ -308,7 +352,7 @@
             V((table, width), BF), V((table, width), BF), V((rows, width), BF),
             V((rows, width), F32), V((rows, 2 * send), BF),
             V((2, half, rpc, cpc), BF), V((half, rpc, cpc), BF), V((half, rpc, cpc), BF),
-            V((half - 1, rpc, cpc), BF), V((2, half, rpc, cpc), BF), dma((8,)), dma,
+            V((half - 1, rpc, cpc), BF), V((2, half, rpc, cpc), BF), dma((8,)), dma((half,)), dma,
         ],
         compiler_params=pltpu.CompilerParams(
             collective_id=0, has_side_effects=True, vmem_limit_bytes=56 * 1024 * 1024
@@ -319,8 +363,9 @@
         msg_bias[None, :], node_bias[None, :], coarse_msg_bias[None, :], coarse_node_bias[None, :],
         fine_nodes, msg_weight, node_weight, coarse_msg_weight, coarse_node_weight, out_grad,
     )
-    ordered = raw.transpose(1, 0, 2, 3).reshape(2 * width // rpc, cut, rpc, cpc).transpose(0, 2, 1, 3)
-    msg_weight_grad = ordered.reshape(2 * width, width).astype(F32) * factor[0, 0]
+    if cut > 1:
+        raw = raw.reshape(2 * width // rpc, cut, rpc, cpc).transpose(0, 2, 1, 3)
+    msg_weight_grad = raw.reshape(2 * width, width).astype(F32) * factor
     return new_fine, new_coarse, node_grad, msg_weight_grad
 
 

time: 65.6 us -> 63.6 us (0.970)
  the two profiles are of different devices: /device:TPU:29 before, /device:TPU:1 now
where the time goes in v2:
time: 63.6 us; the launch traced here: 63.5 us
  Pallas kernels  56.3 us (89%)
  other arithmetic  2.93 us (5%)
  local copies, waits for them, and re-layouts  2.25 us (4%)
  between operations  1.96 us (3%)
    pallas_call x1, Pallas kernels, shards(): pl.pallas_call(functools.partial(layer_kernel, patches, subs, cut), out_s...  56.3 us
    mul x1, other arithmetic, shards(): msg_weight_grad = raw.reshape(2 * width, width).astype(F32) * factor  2.93 us
    unnamed x9, local copies, waits for them, and re-layouts  2.25 us

profile of v2, /device:TPU:1, one launch (start us, length us, event | category | flops | bytes accessed | tf_op | source)
XLA Modules:
  0.0 63.5 jit_solution(10152224164642124173)
XLA Ops:
  1.9 56.3 %layer.1 = (bf16[512,512]{1,0:T(8,128)(2,1)}, bf16[128,512]{1,0:T(8,128)(2,1)}, bf16[512,512]{1,0:T(8,128)(2,1)}, bf16[2,16,32,512]{3,2,1,0:T(8,128)(2,1)}, f32[1,512]{1,0:T(1,128)}) custom-call(s32[1]{0:T(128)S(6)} %copy.24.real_ref, s32[1]{0:T(128)S(6)} %copy.25.live_ref, s32[6,512]{1,0:T(8,128)} %nb_ref.1, s32[2,128]{1,0:T(2,128)} %bitcast.16, ...), custom_call_target="tpu_custom_call" | custom-call | tf_op jit(solution)/shard_map/layer/pallas_call | solution.py:335
  58.3 0.0 copy-start.1
  58.3 0.0 copy-start.2
  58.3 0.0 copy-start
  58.3 2.9 %convert_multiply_fusion = f32[1024,512]{1,0:T(8,128)} fusion(bf16[2,16,32,512]{3,2,1,0:T(8,128)(2,1)} %get-tuple-element.12, f32[512]{0:T(512)} %bitcast.15), kind=kLoop, calls=%fused_computation | loop fusion | flops 1048576 | bytes 3147776 | tf_op jit(solution)/shard_map/mul | solution.py:368
  61.2 0.0 copy-done.1
  61.2 0.8 %copy.26 = bf16[512,512]{1,0:T(8,128)(2,1)} copy(bf16[512,512]{1,0:T(8,128)(2,1)S(1)} %copy-done.1) | data formatting | bytes 1048576
  62.0 0.0 copy-done.2
  62.0 0.7 %copy.27 = bf16[128,512]{1,0:T(8,128)(2,1)} copy(bf16[128,512]{1,0:T(8,128)(2,1)S(1)} %copy-done.2) | data formatting | bytes 262144
  62.7 0.0 copy-done
  62.7 0.8 %copy.28 = bf16[512,512]{1,0:T(8,128)(2,1)} copy(bf16[512,512]{1,0:T(8,128)(2,1)S(1)} %copy-done) | data formatting | bytes 1048576
Async XLA Ops:
  58.3 3.0 %copy-start.1 = (bf16[512,512]{1,0:T(8,128)(2,1)S(1)}, bf16[512,512]{1,0:T(8,128)(2,1)}, u32[]{:S(2)}) copy-start(bf16[512,512]{1,0:T(8,128)(2,1)} %get-tuple-element.18) | copy-start | bytes 1572868
  58.3 3.7 %copy-start.2 = (bf16[128,512]{1,0:T(8,128)(2,1)S(1)}, bf16[128,512]{1,0:T(8,128)(2,1)}, u32[]{:S(2)}) copy-start(bf16[128,512]{1,0:T(8,128)(2,1)} %get-tuple-element.19) | copy-start | bytes 393220
  58.3 4.4 %copy-start = (bf16[512,512]{1,0:T(8,128)(2,1)S(1)}, bf16[512,512]{1,0:T(8,128)(2,1)}, u32[]{:S(2)}) copy-start(bf16[512,512]{1,0:T(8,128)(2,1)} %get-tuple-element.20) | copy-start | bytes 1572868

commit v3 on v2

--- a/solution.py
+++ b/solution.py
@@ -45,7 +45,7 @@
     outgoing, ret, retout, halo_ssem, halo_rsem,
     cbuf, crecv, cag, c_sem,
     pick, slopes, edelta, source, tdelta, dsum, local, sends_oh,
-    gbuf, recv_a, sum_b, recv_b, ag, g_sem, ag_sem, out_sem,
+    gbuf, recv_a, sum_b, recv_b, sum_c, recv_c, ag, g_sem, ag_sem, out_sem,
 ):
     n = patches * subs
     half = n // 2
@@ -58,7 +58,9 @@
     crow, ccol = cbuf.shape[1:]
     me = lax.axis_index("patch") * subs + lax.axis_index("sub")
     par = lax.rem(me, 2)
-    group = lax.div(me, 2)
+    lo = ag_sem.shape[0]
+    hi = half // lo
+    high, low = lax.div(me, 2 * lo), lax.rem(lax.div(me, 2), lo)
 
     def dev(i):
         return (lax.div(i, subs), lax.rem(i, subs))
@@ -206,35 +208,54 @@
         swap.wait_recv()
         sum_b[...] = (gbuf[which].astype(F32) + recv_a[...].astype(F32)).astype(BF)
 
+        for o in range(1, lo):
+            to = lax.rem(low + o, lo)
+            remote(
+                sum_b.at[pl.ds(to * hi, hi)], recv_b.at[o - 1],
+                g_sem.at[2], g_sem.at[3], dev(2 * (high * lo + to) + par),
+            ).start()
+
+    def line(which):
+        remote(recv_b, recv_b, g_sem.at[2], g_sem.at[3], partner).wait_recv()
+        own = sum_b[pl.ds(low * hi, hi)].astype(F32) + jnp.sum(recv_b[...].astype(F32), axis=0)
+        sum_c[...] = own.astype(BF)
+
         def send_chunk(o, c):
-            to = lax.rem(group + o, half)
-            remote(sum_b.at[to], recv_b.at[o - 1], g_sem.at[2], g_sem.at[3], dev(2 * to + par)).start()
+            to = lax.rem(high + o, hi)
+            remote(
+                sum_c.at[to], recv_c.at[o - 1],
+                g_sem.at[7], g_sem.at[8], dev(2 * (to * lo + low) + par),
+            ).start()
             return c
 
-        lax.fori_loop(1, half, send_chunk, 0)
+        lax.fori_loop(1, hi, send_chunk, 0)
 
     def reduce(which):
-        remote(recv_b, recv_b, g_sem.at[2], g_sem.at[3], partner).wait_recv()
-        chunk = jnp.sum(recv_b[...].astype(F32), axis=0) + sum_b[group].astype(F32)
-        ag[which, group] = chunk.astype(BF)
-        mine = ag.at[which, group]
-        remote(mine, mine, g_sem.at[5], g_sem.at[6], partner).start()
+        remote(recv_c, recv_c, g_sem.at[7], g_sem.at[8], partner).wait_recv()
+        chunk = jnp.sum(recv_c[...].astype(F32), axis=0) + sum_c[high].astype(F32)
+        mine = ag.at[which, low * hi + high]
+        ag[which, low * hi + high] = chunk.astype(BF)
 
         def send_sum(o, c):
-            to = lax.rem(group + o, half)
-            remote(mine, mine, g_sem.at[4], ag_sem.at[o], dev(2 * to + par)).start()
+            to = lax.rem(high + o, hi)
+            remote(mine, mine, g_sem.at[4], g_sem.at[9], dev(2 * (to * lo + low) + par)).start()
             return c
 
-        lax.fori_loop(1, half, send_sum, 0)
+        lax.fori_loop(1, hi, send_sum, 0)
+
+    def spread(which):
+        remote(recv_c, recv_c, g_sem.at[4], g_sem.at[9], partner).wait_recv()
+        block = ag.at[which, pl.ds(low * hi, hi)]
+        for o in range(1, lo):
+            to = lax.rem(low + o, lo)
+            remote(block, block, g_sem.at[10], ag_sem.at[o], dev(2 * (high * lo + to) + par)).start()
+        remote(block, block, g_sem.at[5], g_sem.at[6], partner).start()
 
     def forward(which):
-        def pass_on(o, c):
-            got = ag.at[which, lax.rem(group + half - o, half)]
-            remote(got, got, g_sem.at[4], ag_sem.at[o], partner).wait_recv()
+        for o in range(1, lo):
+            got = ag.at[which, pl.ds(lax.rem(low + lo - o, lo) * hi, hi)]
+            remote(got, got, g_sem.at[10], ag_sem.at[o], partner).wait_recv()
             remote(got, got, g_sem.at[5], g_sem.at[6], partner).start()
-            return c
-
-        lax.fori_loop(1, half, pass_on, 0)
 
     odd, even = par == 1, par == 0
     keep(mm_tn(fine, dsum[...]).astype(BF), 1)
@@ -264,6 +285,7 @@
     @pl.when(odd)
     def _():
         swap.start()
+        line(1)
 
     local[...] = out_grad + mm_nt(node_delta, nodew[:width, :])
 
@@ -275,7 +297,17 @@
     def _():
         reduce(1)
 
-    grad = local[...] + mm_nt(dsum[...], msgw[width:, :]) + mm_nt(tdelta[pl.ds(0, rows), :], msgw[:width, :])
+    local[...] += mm_nt(dsum[...], msgw[width:, :])
+    grad = local[...] + mm_nt(tdelta[pl.ds(0, rows), :], msgw[:width, :])
+
+    @pl.when(odd)
+    def _():
+        spread(1)
+
+    @pl.when(even)
+    def _():
+        line(0)
+
     for copy in give:
         copy.wait_recv()
     grad = grad + mm(sends_oh[:, :send], ret[0]) + mm(sends_oh[:, send:], ret[1])
@@ -284,6 +316,7 @@
     @pl.when(even)
     def _():
         reduce(0)
+        spread(0)
         forward(0)
 
     @pl.when(odd)
@@ -304,7 +337,9 @@
     remote(crecv, crecv, c_sem.at[2], c_sem.at[3], partner).wait_send()
     swap.wait_send()
     remote(recv_b, recv_b, g_sem.at[2], g_sem.at[3], partner).wait_send()
-    remote(recv_b, recv_b, g_sem.at[4], g_sem.at[3], partner).wait_send()
+    remote(recv_c, recv_c, g_sem.at[7], g_sem.at[8], partner).wait_send()
+    remote(recv_c, recv_c, g_sem.at[4], g_sem.at[9], partner).wait_send()
+    remote(recv_b, recv_b, g_sem.at[10], g_sem.at[3], partner).wait_send()
     whole_half.wait_send()
     out.wait()
 
@@ -318,6 +353,8 @@
 ):
     n = patches * subs
     half = n // 2
+    lo = 4
+    hi = half // lo
     rows, width = fine_nodes.shape
     send = send_rows.shape[2]
     table = rows + 2 * send
@@ -352,7 +389,7 @@
             V((table, width), BF), V((table, width), BF), V((rows, width), BF),
             V((rows, width), F32), V((rows, 2 * send), BF),
             V((2, half, rpc, cpc), BF), V((half, rpc, cpc), BF), V((half, rpc, cpc), BF),
-            V((half - 1, rpc, cpc), BF), V((2, half, rpc, cpc), BF), dma((8,)), dma((half,)), dma,
+            V((lo - 1, hi, rpc, cpc), BF), V((hi, rpc, cpc), BF), V((hi - 1, rpc, cpc), BF), V((2, half, rpc, cpc), BF), dma((11,)), dma((lo,)), dma,
         ],
         compiler_params=pltpu.CompilerParams(
             collective_id=0, has_side_effects=True, vmem_limit_bytes=56 * 1024 * 1024

time: 63.6 us -> 60.8 us (0.956)
  Pallas kernels: 56.3 us -> 53.5 us
    pallas_call x1, Pallas kernels: 56.3 us -> 53.5 us  [shards(): pl.pallas_call(functools.partial(layer_kernel, patches, subs, cut), out_s...]
where the time goes in v3:
time: 60.8 us; the launch traced here: 60.6 us
  Pallas kernels  53.5 us (88%)
  other arithmetic  2.93 us (5%)
  local copies, waits for them, and re-layouts  2.25 us (4%)
  between operations  1.96 us (3%)
    pallas_call x1, Pallas kernels, shards(): pl.pallas_call(functools.partial(layer_kernel, patches, subs, cut), out_s...  53.5 us
    mul x1, other arithmetic, shards(): msg_weight_grad = raw.reshape(2 * width, width).astype(F32) * factor  2.93 us
    unnamed x9, local copies, waits for them, and re-layouts  2.25 us

profile of v3, /device:TPU:1, one launch (start us, length us, event | category | flops | bytes accessed | tf_op | source)
XLA Modules:
  0.0 60.6 jit_solution(14311733541159052735)
XLA Ops:
  1.9 53.5 %layer.1 = (bf16[512,512]{1,0:T(8,128)(2,1)}, bf16[128,512]{1,0:T(8,128)(2,1)}, bf16[512,512]{1,0:T(8,128)(2,1)}, bf16[2,16,32,512]{3,2,1,0:T(8,128)(2,1)}, f32[1,512]{1,0:T(1,128)}) custom-call(s32[1]{0:T(128)S(6)} %copy.24.real_ref, s32[1]{0:T(128)S(6)} %copy.25.live_ref, s32[6,512]{1,0:T(8,128)} %nb_ref.1, s32[2,128]{1,0:T(2,128)} %bitcast.16, ...), custom_call_target="tpu_custom_call" | custom-call | tf_op jit(solution)/shard_map/layer/pallas_call | solution.py:372
  55.4 0.0 copy-start.1
  55.4 0.0 copy-start.2
  55.5 0.0 copy-start
  55.5 2.9 %convert_multiply_fusion = f32[1024,512]{1,0:T(8,128)} fusion(bf16[2,16,32,512]{3,2,1,0:T(8,128)(2,1)} %get-tuple-element.12, f32[512]{0:T(512)} %bitcast.15), kind=kLoop, calls=%fused_computation | loop fusion | flops 1048576 | bytes 3147776 | tf_op jit(solution)/shard_map/mul | solution.py:405
  58.4 0.0 copy-done.1
  58.4 0.8 %copy.26 = bf16[512,512]{1,0:T(8,128)(2,1)} copy(bf16[512,512]{1,0:T(8,128)(2,1)S(1)} %copy-done.1) | data formatting | bytes 1048576
  59.2 0.0 copy-done.2
  59.2 0.7 %copy.27 = bf16[128,512]{1,0:T(8,128)(2,1)} copy(bf16[128,512]{1,0:T(8,128)(2,1)S(1)} %copy-done.2) | data formatting | bytes 262144
  59.8 0.0 copy-done
  59.9 0.8 %copy.28 = bf16[512,512]{1,0:T(8,128)(2,1)} copy(bf16[512,512]{1,0:T(8,128)(2,1)S(1)} %copy-done) | data formatting | bytes 1048576
Async XLA Ops:
  55.4 3.0 %copy-start.1 = (bf16[512,512]{1,0:T(8,128)(2,1)S(1)}, bf16[512,512]{1,0:T(8,128)(2,1)}, u32[]{:S(2)}) copy-start(bf16[512,512]{1,0:T(8,128)(2,1)} %get-tuple-element.18) | copy-start | bytes 1572868
  55.4 3.7 %copy-start.2 = (bf16[128,512]{1,0:T(8,128)(2,1)S(1)}, bf16[128,512]{1,0:T(8,128)(2,1)}, u32[]{:S(2)}) copy-start(bf16[128,512]{1,0:T(8,128)(2,1)} %get-tuple-element.19) | copy-start | bytes 393220
  55.5 4.4 %copy-start = (bf16[512,512]{1,0:T(8,128)(2,1)S(1)}, bf16[512,512]{1,0:T(8,128)(2,1)}, u32[]{:S(2)}) copy-start(bf16[512,512]{1,0:T(8,128)(2,1)} %get-tuple-element.20) | copy-start | bytes 1572868
